TPU v7x, 256 devices: a whole 4x4x8 slice. The times are simulated.
256 devices in a mesh: grp: 8 (over y, core), mem: 32 (over x, z).
Axes of the slice: x: 4, y: 4, z: 8, core: 2. Of those that a mesh axis runs over, the one named last changes fastest.
Arguments:
- old_rows: bfloat16 [65536, 1024], P(('grp', 'mem')), may hold values from -24 to 24
- new_rows: bfloat16 [65536, 1024], P(('grp', 'mem')), may hold values from -6 to 6
- list_ids: int32 [65536], P(('grp', 'mem')), may hold values from 0 to 65535, as said below
- owner_map: int32 [65536], replicated, may hold values from 0 to 31, as said below
Outputs:
- owner_rows: float32 [131072, 1024], P(('grp', 'mem'))
- rotation: bfloat16 [1024, 1024], P('mem')
Inputs may be any that keep to these rules, and one draw needn't show every extreme that they name: `list_ids`: in each device's block of 256 rows, at most 16 rows belong to lists of any one owner; in every group some owner receives exactly 16 rows from every device of the group. `owner_map`: every owner holds 65536 // 32 lists.
All inputs are finite; a program needn't handle non-finite values.
Results may differ from a plain program's by a relative error of at most 0.023.
Values may be sent and summed in bfloat16 or wider, within the bound.
No kernel may reach another device: no remote copies, remote signals or barrier semaphores. Data moves between devices by JAX's collectives and lax.ppermute only.
A program may use at most 64 MiB of HBM per device.

v0:
```python
import math
import jax
import jax.numpy as jnp
from jax import lax
from jax.sharding import PartitionSpec as P

ITERS = 2
EPSILON = 1e-06
COEFF_ONE = 3.4445
COEFF_THREE = -4.775
COEFF_FIVE = 2.0315


def combine_terms(iterate, first, second):
    return (
        COEFF_ONE * iterate.astype(jnp.float32)
        + COEFF_THREE * first.astype(jnp.float32)
        + COEFF_FIVE * second
    ).astype(jnp.bfloat16)


def local(old_rows, new_rows, list_ids, owner_map):
    features = old_rows.shape[1]
    row_total = old_rows.shape[0]
    members = lax.axis_size("mem")
    block_rows = features // members
    scaling = 0.25 * math.sqrt(features)
    partial_value = jnp.dot(old_rows.T, new_rows, preferred_element_type=jnp.float32)
    covariance = lax.psum(partial_value, ("grp", "mem"))
    squares = jnp.sum(covariance * covariance)
    iterate = (covariance * scaling / jnp.sqrt(squares + EPSILON)).astype(jnp.bfloat16)
    for sweep in range(ITERS):
        gram = jnp.dot(iterate, iterate.T, preferred_element_type=jnp.float32).astype(jnp.bfloat16)
        first = jnp.dot(gram, iterate, preferred_element_type=jnp.float32).astype(jnp.bfloat16)
        second = jnp.dot(gram, first, preferred_element_type=jnp.float32)
        iterate = combine_terms(iterate, first, second)
    own_rows = lax.dynamic_slice_in_dim(iterate, lax.axis_index("mem") * block_rows, block_rows, 0)
    capacity = 2 * row_total // members
    owner_of_row = owner_map[list_ids]
    onehot = (owner_of_row[:, None] == jnp.arange(members, dtype=jnp.int32)[None, :]).astype(
        jnp.int32
    )
    earlier = jnp.cumsum(onehot, axis=0) - onehot
    slot_index = owner_of_row * capacity + jnp.sum(earlier * onehot, axis=1)
    payload = jnp.dot(old_rows, iterate, preferred_element_type=jnp.float32)
    buffer = jnp.zeros((members * capacity, features), jnp.float32).at[slot_index].set(payload)
    buffer = buffer.reshape(members, capacity, features)
    arrived = lax.all_to_all(buffer, "mem", split_axis=0, concat_axis=0, tiled=True).reshape(
        members * capacity, features
    )
    return (arrived, own_rows)


def solution(mesh):
    in_specs = (P(("grp", "mem"), None), P(("grp", "mem"), None), P(("grp", "mem")), P())
    out_specs = (P(("grp", "mem"), None), P("mem", None))
    return jax.shard_map(local, mesh=mesh, in_specs=in_specs, out_specs=out_specs, check_vma=False)
```

profile of v0, /device:TPU:64, one launch (start us, length us, event | category | flops | bytes accessed | tf_op | source)
XLA Modules:
  0.0 378.5 jit_solution(7004765975214528384)
XLA Ops:
  7.2 1.0 copy-done
  8.2 3.8 fusion.8
  12.0 0.7 copy-done.3
  12.7 0.3 copy-done.2
  12.9 1.7 gather_fusion
  14.7 0.6 reduce-window.6
  15.3 0.2 slice_reduce_fusion
  15.6 265.5 %all-reduce.2.cloned.1.call-done = f32[1024,1024]{1,0:T(8,128)} async-done(((f32[1024,1024]{1,0:T(8,128)}), f32[1024,1024]{1,0:T(8,128)}) %all-reduce.2.cloned.1.call-update) | async-done | bytes 4194320 | tf_op jit(solution)/shard_map/psum | solution.py:29
  281.1 3.9 %multiply_reduce_fusion = f32[]{:T(128)} fusion(f32[1024,1024]{1,0:T(8,128)} %all-reduce.2.cloned.1.call-done), kind=kLoop, calls=%fused_computation.5 | loop fusion | flops 2097151 | bytes 4194308 | tf_op jit(solution)/shard_map/reduce_sum | solution.py:30
  285.7 2.8 divide_convert_fusion
  288.5 2.4 convolution_convert_fusion.1
  290.9 2.3 fusion.9
  293.2 2.6 add_convert_fusion.1
  295.8 2.4 convolution_convert_fusion
  298.2 2.3 fusion.10
  300.5 2.8 add_convert_fusion
  303.3 1.3 copy-done.1
  304.7 0.8 convolution_bitcast_fusion
  305.5 0.3 copy.8
  305.8 2.8 scatter_custom_fusion
  308.6 11.8 %all-to-all-start = ((f32[32,16,1024]{2,1,0:T(8,128)}), f32[32,16,1024]{2,1,0:T(8,128)S(1)}, u32[]{:S(2)}, u32[]{:S(2)}) async-start(f32[32,16,1024]{2,1,0:T(8,128)} %bitcast.43), calls=%async_computation | async-start | bytes 4194304 | tf_op jit(solution)/shard_map/all_to_all | solution.py:48
  320.4 1.5 constant_dynamic-slice_fusion
  321.9 48.5 %all-to-all-done = f32[32,16,1024]{2,1,0:T(8,128)S(1)} async-done(((f32[32,16,1024]{2,1,0:T(8,128)}), f32[32,16,1024]{2,1,0:T(8,128)S(1)}, u32[]{:S(2)}, u32[]{:S(2)}) %all-to-all-start) | async-done | bytes 2097184 | tf_op jit(solution)/shard_map/all_to_all | solution.py:48
  370.4 1.3 copy.13
  (14 shorter events, 0.2 us)
Async XLA Ops:
  7.2 1.0 copy-start
  7.2 273.9 %all-reduce.2.cloned.1.call-start = ((), (), s32[]{:S(2)}) async-start(), calls=%async_computation.1 | async-start | bytes 8388608 | tf_op jit(solution)/shard_map/psum | solution.py:29
  12.0 0.7 copy-start.3
  12.0 1.0 copy-start.2
  303.3 1.4 copy-start.1
  308.6 61.7 %all-to-all-start = ((f32[32,16,1024]{2,1,0:T(8,128)}), f32[32,16,1024]{2,1,0:T(8,128)S(1)}, u32[]{:S(2)}, u32[]{:S(2)}) async-start(f32[32,16,1024]{2,1,0:T(8,128)} %bitcast.43), calls=%async_computation | async-start | bytes 4194304 | tf_op jit(solution)/shard_map/all_to_all | solution.py:48
Sparse Core Ops, SparseCore 0:
  13.5 267.5 all-reduce.1
where the time goes:
time: 379 us
  waiting for transfers between devices  314 us (83%)
  matrix products  19.3 us (5%)
  between operations  14.9 us (4%)
  starting transfers between devices  11.8 us (3%)
  local copies, waits for them, and re-layouts  11.1 us (3%)
  other arithmetic  7.41 us (2%)
    psum x1, waiting for transfers between devices, local(): covariance = lax.psum(partial_value, ('grp', 'mem'))  265 us
    all_to_all x1, waiting for transfers between devices, local(): lax.all_to_all(buffer, 'mem', split_axis=0, concat_axis=0, tiled=True)  48.5 us
    all_to_all x1, starting transfers between devices, local(): lax.all_to_all(buffer, 'mem', split_axis=0, concat_axis=0, tiled=True)  11.8 us
  transfers between devices with their start and end apart: 2, of which 2 were waited for; matrix products, arithmetic and copies ran while one was open for 1% of the time, Pallas kernels for 0%

commit v1 on v0

--- a/solution.py
+++ b/solution.py
@@ -26,7 +26,9 @@
     block_rows = features // members
     scaling = 0.25 * math.sqrt(features)
     partial_value = jnp.dot(old_rows.T, new_rows, preferred_element_type=jnp.float32)
-    covariance = lax.psum(partial_value, ("grp", "mem"))
+    covariance = partial_value
+    for hop_no in ("mem", "grp"):
+        covariance = jax.lax.psum(covariance, hop_no)
     squares = jnp.sum(covariance * covariance)
     iterate = (covariance * scaling / jnp.sqrt(squares + EPSILON)).astype(jnp.bfloat16)
     for sweep in range(ITERS):

time: 379 us -> 351 us (0.926)
  waiting for transfers between devices: 314 us -> 286 us
    psum x1 -> x2, waiting for transfers between devices: 265 us -> 240 us  [local(): covariance = jax.lax.psum(covariance, hop_no)]
  transfers between devices with their start and end apart: 2 -> 3, of which waited for: 2 -> 3; matrix products, arithmetic and copies ran while one was open for 1% -> 1% of each run, Pallas kernels for 0% -> 0%
where the time goes in v1:
time: 351 us; the launch traced here: 349 us
  waiting for transfers between devices  286 us (81%)
  matrix products  19.4 us (6%)
  between operations  14.9 us (4%)
  local copies, waits for them, and re-layouts  11.1 us (3%)
  starting transfers between devices  10 us (3%)
  other arithmetic  7.41 us (2%)
    psum x2, waiting for transfers between devices, local(): covariance = jax.lax.psum(covariance, hop_no)  240 us
    all_to_all x1, waiting for transfers between devices, local(): lax.all_to_all(buffer, 'mem', split_axis=0, concat_axis=0, tiled=True)  45.9 us
    all_to_all x1, starting transfers between devices, local(): lax.all_to_all(buffer, 'mem', split_axis=0, concat_axis=0, tiled=True)  9.97 us
  transfers between devices with their start and end apart: 3, of which 3 were waited for; matrix products, arithmetic and copies ran while one was open for 1% of the time, Pallas kernels for 0%

profile of v1, /device:TPU:64, one launch (start us, length us, event | category | flops | bytes accessed | tf_op | source)
XLA Modules:
  0.0 348.9 jit_solution(9694412791120650395)
XLA Ops:
  7.2 1.0 copy-done
  8.2 3.8 %fusion.8 = f32[1024,1024]{1,0:T(8,128)} fusion(bf16[256,1024]{1,0:T(8,128)(2,1)S(1)} %copy-done, bf16[256,1024]{1,0:T(8,128)(2,1)} %param.5), kind=kOutput, calls=%fused_computation.27 | convolution fusion | flops 536870912 | bytes 5242880 | tf_op jit(solution)/shard_map/dot_general | solution.py:28
  12.0 165.9 %all-reduce.3.cloned.1.call-done = f32[1024,1024]{1,0:T(8,128)} async-done(((f32[1024,1024]{1,0:T(8,128)}), f32[1024,1024]{1,0:T(8,128)}) %all-reduce.3.cloned.1.call-update) | async-done | bytes 4194320 | tf_op jit(solution)/shard_map/psum | solution.py:31
  178.0 0.7 copy-done.3
  178.7 0.3 copy-done.2
  179.0 1.7 gather_fusion
  180.7 0.6 reduce-window.6
  181.6 74.2 %all-reduce.5.cloned.1.call-done = f32[1024,1024]{1,0:T(8,128)} async-done(((f32[1024,1024]{1,0:T(8,128)}), f32[1024,1024]{1,0:T(8,128)}) %all-reduce.5.cloned.1.call-update) | async-done | bytes 4194320 | tf_op jit(solution)/shard_map/psum | solution.py:31
  255.9 3.9 %multiply_reduce_fusion = f32[]{:T(128)} fusion(f32[1024,1024]{1,0:T(8,128)} %all-reduce.5.cloned.1.call-done), kind=kLoop, calls=%fused_computation.5 | loop fusion | flops 2097151 | bytes 4194308 | tf_op jit(solution)/shard_map/reduce_sum | solution.py:32
  260.4 2.8 divide_convert_fusion
  263.2 2.4 convolution_convert_fusion.1
  265.6 2.3 fusion.9
  267.9 2.6 add_convert_fusion.1
  270.6 2.4 convolution_convert_fusion
  272.9 2.3 fusion.10
  275.3 2.8 add_convert_fusion
  278.1 1.3 copy-done.1
  279.5 0.8 convolution_bitcast_fusion
  280.2 0.3 copy.8
  280.6 2.8 scatter_custom_fusion
  283.4 10.0 %all-to-all-start = ((f32[32,16,1024]{2,1,0:T(8,128)}), f32[32,16,1024]{2,1,0:T(8,128)S(1)}, u32[]{:S(2)}, u32[]{:S(2)}) async-start(f32[32,16,1024]{2,1,0:T(8,128)} %bitcast.43), calls=%async_computation | async-start | bytes 4194304 | tf_op jit(solution)/shard_map/all_to_all | solution.py:50
  293.4 1.5 constant_dynamic-slice_fusion
  294.9 45.9 %all-to-all-done = f32[32,16,1024]{2,1,0:T(8,128)S(1)} async-done(((f32[32,16,1024]{2,1,0:T(8,128)}), f32[32,16,1024]{2,1,0:T(8,128)S(1)}, u32[]{:S(2)}, u32[]{:S(2)}) %all-to-all-start) | async-done | bytes 2097184 | tf_op jit(solution)/shard_map/all_to_all | solution.py:50
  340.7 1.3 copy.14
  (17 shorter events, 0.5 us)
Async XLA Ops:
  7.2 1.0 copy-start
  7.2 170.8 %all-reduce.3.cloned.1.call-start = ((), (), s32[]{:S(2)}) async-start(), calls=%async_computation.1 | async-start | bytes 8388608 | tf_op jit(solution)/shard_map/psum | solution.py:31
  12.0 243.9 %all-reduce.5.cloned.1.call-start = ((), (), s32[]{:S(2)}) async-start(), calls=%async_computation.2 | async-start | bytes 8388608 | tf_op jit(solution)/shard_map/psum | solution.py:31
  178.0 0.7 copy-start.3
  178.0 1.0 copy-start.2
  278.1 1.4 copy-start.1
  283.4 57.3 %all-to-all-start = ((f32[32,16,1024]{2,1,0:T(8,128)}), f32[32,16,1024]{2,1,0:T(8,128)S(1)}, u32[]{:S(2)}, u32[]{:S(2)}) async-start(f32[32,16,1024]{2,1,0:T(8,128)} %bitcast.43), calls=%async_computation | async-start | bytes 4194304 | tf_op jit(solution)/shard_map/all_to_all | solution.py:50
Sparse Core Ops, SparseCore 0:
  12.1 165.8 all-reduce.2
  180.5 75.3 all-reduce.4
